TPU v7x, 32 devices: a whole 2x2x4 slice. The times are simulated.
32 devices in a mesh: dp: 8 (over z, y), fsdp: 4 (over x, core).
Axes of the slice: x: 2, y: 2, z: 4, core: 2. Of those that a mesh axis runs over, the one named last changes fastest.
Arguments:
- inputs: bfloat16 [16, 1024, 1024], P('dp', 'fsdp'), may hold values from -6 to 6
- timestep: int32 [16], P('dp'), may hold values from 0 to 4999, as said below
- bucket_count: int32 [8], replicated, may hold values from 1 to 2, as said below
- upstream: bfloat16 [16, 1024, 1024], P('dp', 'fsdp'), may hold values from -6 to 6
- query_weight: bfloat16 [1024, 1024], P('fsdp'), may hold values from -0.1875 to 0.1875
- key_weight: bfloat16 [1024, 1024], P('fsdp'), may hold values from -0.1875 to 0.1875
- value_weight: bfloat16 [1024, 1024], P('fsdp'), may hold values from -0.1875 to 0.1875
- output_weight: bfloat16 [1024, 1024], P('fsdp'), may hold values from -1 to 1
- up_weight: bfloat16 [1024, 4096], P('fsdp'), may hold values from -0.1875 to 0.1875
- down_weight: bfloat16 [4096, 1024], P('fsdp'), may hold values from -0.09375 to 0.09375
- query_bias: bfloat16 [1024], P('fsdp'), may hold values from -2 to 2
- value_bias: bfloat16 [1024], P('fsdp'), may hold values from -2 to 2
- output_bias: bfloat16 [1024], P('fsdp'), may hold values from -2 to 2
- up_bias: bfloat16 [4096], P('fsdp'), may hold values from -2 to 2
- down_bias: bfloat16 [1024], P('fsdp'), may hold values from -2 to 2
- first_gain: bfloat16 [1024], P('fsdp'), may hold values from 0.5 to 1.5
- first_shift: bfloat16 [1024], P('fsdp'), may hold values from -2 to 2
- second_gain: bfloat16 [1024], P('fsdp'), may hold values from 0.5 to 1.5
- second_shift: bfloat16 [1024], P('fsdp'), may hold values from -2 to 2
Outputs:
- activations: bfloat16 [16, 1024, 1024], P('dp', 'fsdp')
- input_gradient: float32 [16, 1024, 1024], P('dp', 'fsdp')
- time_gradient: float32 [16, 1024], P('dp', 'fsdp')
- query_weight_gradient: float32 [1024, 1024], P('fsdp')
- key_weight_gradient: float32 [1024, 1024], P('fsdp')
- value_weight_gradient: float32 [1024, 1024], P('fsdp')
- output_weight_gradient: float32 [1024, 1024], P('fsdp')
- up_weight_gradient: float32 [1024, 4096], P('fsdp')
- down_weight_gradient: float32 [4096, 1024], P('fsdp')
- query_bias_gradient: float32 [1024], P('fsdp')
- value_bias_gradient: float32 [1024], P('fsdp')
- output_bias_gradient: float32 [1024], P('fsdp')
- up_bias_gradient: float32 [4096], P('fsdp')
- down_bias_gradient: float32 [1024], P('fsdp')
- first_gain_gradient: float32 [1024], P('fsdp')
- first_shift_gradient: float32 [1024], P('fsdp')
- second_gain_gradient: float32 [1024], P('fsdp')
- second_shift_gradient: float32 [1024], P('fsdp')
Inputs may be any that keep to these rules, and one draw needn't show every extreme that they name: Slots 0 to bucket_count[b] - 1 of bucket b are live, the others carry no gradient; the last bucket is always full. The timestep of sequence s lies in [b W, (b + 1) W) with b = s // 2 and W = 5000 divided by the number of buckets, rounded down.
All inputs are finite; a program needn't handle non-finite values.
Results may differ from a plain program's by a relative error of at most 0.017.
Values may be sent and summed in bfloat16 or wider, within the bound.
No kernel may reach another device: no remote copies, remote signals or barrier semaphores. Data moves between devices by JAX's collectives and lax.ppermute only.
A program may use at most 256 MiB of HBM per device.

v0:
```python
import math

import jax
import jax.numpy as jnp
from jax import lax
from jax.sharding import PartitionSpec as P

D = 1024
HEADS = 16
HEAD_DIM = 64


def sinusoid(timestep):
    halves = D // 2
    frequency = jnp.exp(jnp.arange(halves, dtype=jnp.float32) * (-math.log(10000.0) / halves))
    angles = timestep.astype(jnp.float32)[:, None] * frequency[None, :]
    return jnp.concatenate([jnp.sin(angles), jnp.cos(angles)], axis=1)


def layer_norm(residual, norm_gain, norm_shift):
    row_mean = jnp.mean(residual, axis=-1, keepdims=True)
    centered = residual - row_mean
    row_var = jnp.mean(centered * centered, axis=-1, keepdims=True)
    return centered * lax.rsqrt(row_var + 1e-05) * norm_gain + norm_shift


def gelu_exact(upward):
    return jax.nn.gelu(upward, approximate=False)


def project(rows_in, matrix):
    return jnp.dot(rows_in, matrix, preferred_element_type=jnp.float32)


def project_back(rows_in, matrix):
    return lax.dot_general(
        rows_in, matrix, (((1,), (1,)), ((), ())), preferred_element_type=jnp.float32
    )


def outer_sum(left_side, right_side):
    return lax.dot_general(
        left_side, right_side, (((0,), (0,)), ((), ())), preferred_element_type=jnp.float32
    )


def as_float(vector):
    return vector.astype(jnp.float32)


def front(inputs, embeddings, params):
    block_shape = inputs.shape
    hidden = inputs.astype(jnp.float32) + embeddings[:, None, :]
    rounded = hidden.astype(jnp.bfloat16).reshape(-1, D)
    queries = (project(rounded, params[0]) + as_float(params[6])).astype(jnp.bfloat16)
    key_rows = project(rounded, params[1]).astype(jnp.bfloat16)
    values = (project(rounded, params[2]) + as_float(params[7])).astype(jnp.bfloat16)
    return (
        hidden.reshape(-1, D),
        rounded,
        queries.reshape(block_shape),
        key_rows.reshape(block_shape),
        values.reshape(block_shape),
    )


def attend(operands):
    query_block, key_block, value_block = operands
    query_heads = query_block.reshape(-1, HEADS, HEAD_DIM)
    key_heads = key_block.reshape(-1, HEADS, HEAD_DIM)
    value_heads = value_block.reshape(-1, HEADS, HEAD_DIM)
    scores = jnp.einsum(
        "qhd,khd->hqk", query_heads, key_heads, preferred_element_type=jnp.float32
    ) * HEAD_DIM ** (-0.5)
    row_peak = jnp.max(scores, axis=-1, keepdims=True)
    exponent = jnp.exp(scores - row_peak)
    row_total = jnp.sum(exponent, axis=-1, keepdims=True)
    attention = exponent / row_total
    mixed_rows = jnp.einsum(
        "hqk,khd->qhd",
        attention.astype(jnp.bfloat16),
        value_heads,
        preferred_element_type=jnp.float32,
    )
    return (mixed_rows.reshape(-1, D).astype(jnp.bfloat16), row_peak + jnp.log(row_total))


def attend_back(operands):
    query_block, key_block, value_block, logsum, mixed_grad = operands
    scaling = HEAD_DIM ** (-0.5)
    query_heads = query_block.reshape(-1, HEADS, HEAD_DIM)
    key_heads = key_block.reshape(-1, HEADS, HEAD_DIM)
    value_heads = value_block.reshape(-1, HEADS, HEAD_DIM)
    grad_heads = mixed_grad.reshape(-1, HEADS, HEAD_DIM)
    scores = (
        jnp.einsum("qhd,khd->hqk", query_heads, key_heads, preferred_element_type=jnp.float32)
        * scaling
    )
    attention = jnp.exp(scores - logsum)
    prob_grad = jnp.einsum(
        "qhd,khd->hqk", grad_heads, value_heads, preferred_element_type=jnp.float32
    )
    score_grad = (
        attention * (prob_grad - jnp.sum(attention * prob_grad, axis=-1, keepdims=True))
    ).astype(jnp.bfloat16)
    query_grad = (
        jnp.einsum("hqk,khd->qhd", score_grad, key_heads, preferred_element_type=jnp.float32)
        * scaling
    ).astype(jnp.bfloat16)
    key_part = (
        jnp.einsum("hqk,qhd->khd", score_grad, query_heads, preferred_element_type=jnp.float32)
        * scaling
    )
    value_part = jnp.einsum(
        "hqk,qhd->khd",
        attention.astype(jnp.bfloat16),
        grad_heads,
        preferred_element_type=jnp.float32,
    )
    return (query_grad.reshape(-1, D), key_part.reshape(-1, D), value_part.reshape(-1, D))


def tail(hidden, mixed_rows, params):
    branch = project(mixed_rows, params[3]) + as_float(params[8])
    first_input = hidden + branch
    first_norm = layer_norm(first_input, as_float(params[11]), as_float(params[12]))
    first_low = first_norm.astype(jnp.bfloat16)
    upward = project(first_low, params[4]) + as_float(params[9])
    activated = gelu_exact(upward).astype(jnp.bfloat16)
    second_input = first_norm + (project(activated, params[5]) + as_float(params[10]))
    final_rows = layer_norm(second_input, as_float(params[13]), as_float(params[14]))
    return (final_rows, (first_input, first_low, upward, activated, second_input))


def norm_back(residual, norm_gain, norm_shift, grad_rows):
    unused, pullback = jax.vjp(layer_norm, residual, norm_gain, norm_shift)
    return pullback(grad_rows)


def column_sum(delta):
    return jnp.sum(delta.astype(jnp.float32), axis=0)


def per_device(
    inputs,
    timestep,
    bucket_count,
    upstream,
    query_weight,
    key_weight,
    value_weight,
    output_weight,
    up_weight,
    down_weight,
    query_bias,
    value_bias,
    output_bias,
    up_bias,
    down_bias,
    first_gain,
    first_shift,
    second_gain,
    second_shift,
):
    block_shape = inputs.shape
    sequence_count = block_shape[0]
    params = (
        lax.all_gather(query_weight, "fsdp", axis=0, tiled=True),
        lax.all_gather(key_weight, "fsdp", axis=0, tiled=True),
        lax.all_gather(value_weight, "fsdp", axis=0, tiled=True),
        lax.all_gather(output_weight, "fsdp", axis=0, tiled=True),
        lax.all_gather(up_weight, "fsdp", axis=0, tiled=True),
        lax.all_gather(down_weight, "fsdp", axis=0, tiled=True),
        lax.all_gather(query_bias, "fsdp", axis=0, tiled=True),
        lax.all_gather(value_bias, "fsdp", axis=0, tiled=True),
        lax.all_gather(output_bias, "fsdp", axis=0, tiled=True),
        lax.all_gather(up_bias, "fsdp", axis=0, tiled=True),
        lax.all_gather(down_bias, "fsdp", axis=0, tiled=True),
        lax.all_gather(first_gain, "fsdp", axis=0, tiled=True),
        lax.all_gather(first_shift, "fsdp", axis=0, tiled=True),
        lax.all_gather(second_gain, "fsdp", axis=0, tiled=True),
        lax.all_gather(second_shift, "fsdp", axis=0, tiled=True),
    )
    embeddings = sinusoid(timestep)
    hidden, rounded, queries, key_rows, values = front(inputs, embeddings, params)
    key_all, value_all = (
        lax.all_gather(key_rows, "fsdp", axis=1, tiled=True),
        lax.all_gather(values, "fsdp", axis=1, tiled=True),
    )
    mixed_rows, logsum = lax.map(attend, (queries, key_all, value_all))
    final_rows, stored = tail(hidden, mixed_rows.reshape(-1, D), params)
    activations = final_rows.reshape(block_shape).astype(jnp.bfloat16)
    inputs_again, embeds_again, unused = lax.optimization_barrier((inputs, embeddings, activations))
    params = (
        lax.all_gather(query_weight, "fsdp", axis=0, tiled=True),
        lax.all_gather(key_weight, "fsdp", axis=0, tiled=True),
        lax.all_gather(value_weight, "fsdp", axis=0, tiled=True),
        lax.all_gather(output_weight, "fsdp", axis=0, tiled=True),
        lax.all_gather(up_weight, "fsdp", axis=0, tiled=True),
        lax.all_gather(down_weight, "fsdp", axis=0, tiled=True),
        lax.all_gather(query_bias, "fsdp", axis=0, tiled=True),
        lax.all_gather(value_bias, "fsdp", axis=0, tiled=True),
        lax.all_gather(output_bias, "fsdp", axis=0, tiled=True),
        lax.all_gather(up_bias, "fsdp", axis=0, tiled=True),
        lax.all_gather(down_bias, "fsdp", axis=0, tiled=True),
        lax.all_gather(first_gain, "fsdp", axis=0, tiled=True),
        lax.all_gather(first_shift, "fsdp", axis=0, tiled=True),
        lax.all_gather(second_gain, "fsdp", axis=0, tiled=True),
        lax.all_gather(second_shift, "fsdp", axis=0, tiled=True),
    )
    hidden, rounded, queries, key_rows, values = front(inputs_again, embeds_again, params)
    key_all, value_all = (
        lax.all_gather(key_rows, "fsdp", axis=1, tiled=True),
        lax.all_gather(values, "fsdp", axis=1, tiled=True),
    )
    mixed_rows, logsum = lax.map(attend, (queries, key_all, value_all))
    final_rows, stored = tail(hidden, mixed_rows.reshape(-1, D), params)
    first_input, first_low, upward, activated, second_input = stored
    mixed_flat = mixed_rows.reshape(-1, D)
    slot_index = jnp.arange(sequence_count)
    live_slot = slot_index < bucket_count[lax.axis_index("dp")]
    seq_weight = live_slot.astype(jnp.float32) * (
        sequence_count * lax.axis_size("dp") / jnp.sum(bucket_count).astype(jnp.float32)
    )
    cotangent = (upstream.astype(jnp.float32) * seq_weight[:, None, None]).reshape(-1, D)
    second_grad, second_gain_part, second_shift_part = norm_back(
        second_input, as_float(params[13]), as_float(params[14]), cotangent
    )
    down_delta = second_grad.astype(jnp.bfloat16)
    down_bias_part = column_sum(down_delta)
    unused_up, gelu_pull = jax.vjp(gelu_exact, upward)
    up_delta = gelu_pull(project_back(down_delta, params[5]))[0].astype(jnp.bfloat16)
    up_bias_part = column_sum(up_delta)
    first_grad = second_grad + project_back(up_delta, params[4])
    first_input_grad, first_gain_part, first_shift_part = norm_back(
        first_input, as_float(params[11]), as_float(params[12]), first_grad
    )
    out_delta = first_input_grad.astype(jnp.bfloat16)
    output_bias_part = column_sum(out_delta)
    mixed_grad = project_back(out_delta, params[3]).astype(jnp.bfloat16).reshape(block_shape)
    query_delta, key_part, value_part = lax.map(
        attend_back, (queries, key_all, value_all, logsum, mixed_grad)
    )
    key_delta, value_delta = (
        lax.psum_scatter(key_part, "fsdp", scatter_dimension=1, tiled=True),
        lax.psum_scatter(value_part, "fsdp", scatter_dimension=1, tiled=True),
    )
    query_delta = query_delta.reshape(-1, D)
    key_delta = key_delta.astype(jnp.bfloat16).reshape(-1, D)
    value_delta = value_delta.astype(jnp.bfloat16).reshape(-1, D)
    query_bias_part = column_sum(query_delta)
    value_bias_part = column_sum(value_delta)
    hidden_grad = (
        first_input_grad
        + project_back(query_delta, params[0])
        + project_back(key_delta, params[1])
        + project_back(value_delta, params[2])
    )
    input_gradient = hidden_grad.reshape(block_shape)
    time_part = jnp.sum(input_gradient, axis=1)
    wide_shard = lax.psum_scatter(
        jnp.concatenate(
            [
                outer_sum(rounded, query_delta),
                outer_sum(rounded, key_delta),
                outer_sum(rounded, value_delta),
                outer_sum(mixed_flat, out_delta),
                outer_sum(first_low, up_delta),
            ],
            axis=1,
        ),
        "fsdp",
        scatter_dimension=0,
        tiled=True,
    )
    down_shard = lax.psum_scatter(
        outer_sum(activated, down_delta), "fsdp", scatter_dimension=0, tiled=True
    )
    small_shards = (
        lax.psum_scatter(query_bias_part, "fsdp", scatter_dimension=0, tiled=True),
        lax.psum_scatter(value_bias_part, "fsdp", scatter_dimension=0, tiled=True),
        lax.psum_scatter(output_bias_part, "fsdp", scatter_dimension=0, tiled=True),
        lax.psum_scatter(up_bias_part, "fsdp", scatter_dimension=0, tiled=True),
        lax.psum_scatter(down_bias_part, "fsdp", scatter_dimension=0, tiled=True),
        lax.psum_scatter(first_gain_part, "fsdp", scatter_dimension=0, tiled=True),
        lax.psum_scatter(first_shift_part, "fsdp", scatter_dimension=0, tiled=True),
        lax.psum_scatter(second_gain_part, "fsdp", scatter_dimension=0, tiled=True),
        lax.psum_scatter(second_shift_part, "fsdp", scatter_dimension=0, tiled=True),
        lax.psum_scatter(time_part, "fsdp", scatter_dimension=1, tiled=True),
    )
    summed = lax.psum(
        (
            wide_shard,
            down_shard,
            small_shards[0],
            small_shards[1],
            small_shards[2],
            small_shards[3],
            small_shards[4],
            small_shards[5],
            small_shards[6],
            small_shards[7],
            small_shards[8],
        ),
        "dp",
    )
    wide_total = summed[0]
    return (
        activations,
        input_gradient,
        small_shards[9],
        wide_total[:, 0:D],
        wide_total[:, D : 2 * D],
        wide_total[:, 2 * D : 3 * D],
        wide_total[:, 3 * D : 4 * D],
        wide_total[:, 4 * D :],
        summed[1],
        summed[2],
        summed[3],
        summed[4],
        summed[5],
        summed[6],
        summed[7],
        summed[8],
        summed[9],
        summed[10],
    )


def solution(mesh):
    placed = (
        P("dp", "fsdp", None),
        P("dp"),
        P(),
        P("dp", "fsdp", None),
        P("fsdp", None),
        P("fsdp", None),
        P("fsdp", None),
        P("fsdp", None),
        P("fsdp", None),
        P("fsdp", None),
        P("fsdp"),
        P("fsdp"),
        P("fsdp"),
        P("fsdp"),
        P("fsdp"),
        P("fsdp"),
        P("fsdp"),
        P("fsdp"),
        P("fsdp"),
    )
    return jax.shard_map(
        per_device,
        mesh=mesh,
        in_specs=placed,
        out_specs=(
            P("dp", "fsdp", None),
            P("dp", "fsdp", None),
            P("dp", "fsdp"),
            P("fsdp", None),
            P("fsdp", None),
            P("fsdp", None),
            P("fsdp", None),
            P("fsdp", None),
            P("fsdp", None),
            P("fsdp"),
            P("fsdp"),
            P("fsdp"),
            P("fsdp"),
            P("fsdp"),
            P("fsdp"),
            P("fsdp"),
            P("fsdp"),
            P("fsdp"),
        ),
        check_vma=False,
    )
```

profile of v0, /device:TPU:0, one launch (start us, length us, event | category | flops | bytes accessed | tf_op | source)
XLA Modules:
  0.0 1629.7 jit_solution(11717452708855204383)
XLA Ops:
  20.5 14.5 all-gather.19.cloned.1.call-done
  39.3 19.8 %all-gather.25.cloned.1.call-done = bf16[1024,1024]{1,0:T(8,128)(2,1)} async-done(((bf16[256,1024]{1,0:T(8,128)(2,1)}), bf16[1024,1024]{1,0:T(8,128)(2,1)}) %all-gather.25.cloned.1.call-update) | async-done | bytes 2097168 | tf_op jit(solution)/shard_map/all_gather | solution.py:169
  120.4 37.0 %all-gather.27.cloned.1.call-done = bf16[2,1024,1024]{1,2,0:T(8,128)(2,1)} async-done(((bf16[2,256,1024]{1,2,0:T(8,128)(2,1)}), bf16[2,1024,1024]{1,2,0:T(8,128)(2,1)}) %all-gather.27.cloned.1.call-update) | async-done | bytes 4194320 | tf_op jit(solution)/shard_map/all_gather | solution.py:187
  158.5 48.9 %while.36 = (s32[]{:T(128)}, bf16[2,256,1024]{2,1,0:T(8,128)(2,1)}, bf16[2,1024,1024]{1,2,0:T(8,128)(2,1)}, bf16[2,256,1024]{2,1,0:T(8,128)(2,1)}, bf16[2,1024,1024]{1,2,0:T(8,128)(2,1)}, /*index=5*/s32[]{:T(128)}) while((s32[]{:T(128)}, bf16[2,256,1024]{2,1,0:T(8,128)(2,1)}, bf16[2,1024,1024]{1,2,0:T(8,128)(2,1)}, ...), condition=%wide.region_3.4_spmd, body=%wide.region_0.3_spmd.sunk | while | flops 1094976512 | bytes 55607912 | solution.py:190
  186.6 11.1 fusion.222
  213.0 28.4 %all-gather.31.cloned.1.call-done = bf16[1024,4096]{1,0:T(8,128)(2,1)} async-done(((bf16[256,4096]{1,0:T(8,128)(2,1)}), bf16[1024,4096]{1,0:T(8,128)(2,1)}) %all-gather.31.cloned.1.call-update) | async-done | bytes 8388624 | tf_op jit(solution)/shard_map/all_gather | solution.py:172
  241.4 59.9 %all-gather.33.cloned.1.call-done = bf16[4096,1024]{1,0:T(8,128)(2,1)} async-done(((bf16[1024,1024]{1,0:T(8,128)(2,1)}), bf16[4096,1024]{1,0:T(8,128)(2,1)}) %all-gather.33.cloned.1.call-update) | async-done | bytes 8388624 | tf_op jit(solution)/shard_map/all_gather | solution.py:173
  301.3 32.7 %fusion.126 = (f32[512]{0:T(512)S(1)}, f32[512,1024]{1,0:T(8,128)S(1)}) fusion(f32[1024]{0:T(1024)S(1)} %bitcast.262, bf16[4096,1024]{1,0:T(8,128)(2,1)} %all-gather.33.cloned.1.call-done, bf16[1024,4096]{1,0:T(8,128)(2,1)} %all-gather.31.cloned.1.call-done, f32[4096]{0:T(1024)S(1)} %convert_element_type.191, f32[512,1024]{1,0:T(8,128)} %copy-done.27, ...), kind=kOutput, calls=%fused_computation.220 | convolution fusion | flops 8734638080 | bytes 21006336 | tf_op jit(solution)/shard_map/dot_general | solution.py:32
  352.8 22.6 %all-gather.35.cloned.1.call-done = bf16[2,1024,1024]{1,2,0:T(8,128)(2,1)} async-done(((bf16[2,256,1024]{1,2,0:T(8,128)(2,1)}), bf16[2,1024,1024]{1,2,0:T(8,128)(2,1)}) %all-gather.35.cloned.1.call-update) | async-done | bytes 4194320 | tf_op jit(solution)/shard_map/all_gather | solution.py:214
  375.4 37.0 %all-gather.37.cloned.1.call-done = bf16[2,1024,1024]{1,2,0:T(8,128)(2,1)} async-done(((bf16[2,256,1024]{1,2,0:T(8,128)(2,1)}), bf16[2,1024,1024]{1,2,0:T(8,128)(2,1)}) %all-gather.37.cloned.1.call-update) | async-done | bytes 4194320 | tf_op jit(solution)/shard_map/all_gather | solution.py:213
  412.5 27.4 %while.37 = (s32[]{:T(128)}, bf16[2,256,1024]{2,1,0:T(8,128)(2,1)S(1)}, f32[2,16,256,1]{2,1,3,0:T(8,128)S(1)}, bf16[2,1024,1024]{1,2,0:T(8,128)(2,1)}, bf16[2,25...) while((s32[]{:T(128)}, bf16[2,256,1024]{2,1,0:T(8,128)(2,1)S(1)}, ...), condition=%wide.region_12.13_spmd, body=%wide.region_9.0_spmd.sunk | while | flops 1111748608 | bytes 67240032 | solution.py:216
  445.3 26.2 %multiply_convert_fusion.1 = (bf16[512,4096]{1,0:T(8,128)(2,1)S(1)}, f32[512,4096]{1,0:T(8,128)}, f32[512,4096]{1,0:T(8,128)}) fusion(f32[4096]{0:T(1024)S(1)} %copy-done.50, bf16[1024,4096]{1,0:T(8,128)(2,1)S(1)} %bitcast.269, f32[512,1024]{1,0:T(8,128)S(1)} %get-tuple-element.305, f32[512]{0:T(512)S(1)} %fusion.84, f32[512]{0:T(512)S(1)} %broadcast_multiply_fusion.1, ...), kind=kOutput, calls=%fused_computation.54 | convolution fusion | flops 4436000768 | bytes 31485952 | tf_op jit(solution)/shard_map/dot_general | solution.py:32
  479.7 15.6 convert_reduce_fusion
  510.9 161.2 %while.38 = (s32[]{:T(128)}, bf16[2,256,1024]{1,2,0:T(8,128)(2,1)}, f32[2,1024,1024]{2,1,0:T(8,128)}, f32[2,1024,1024]{2,1,0:T(8,128)}, bf16[2,1024,1024]{1,2,0:...) while((s32[]{:T(128)}, bf16[2,256,1024]{1,2,0:T(8,128)(2,1)}, ...), condition=%wide.region_23.24_spmd, body=%wide.region_21.23_spmd.sunk | while | flops 2736254976 | bytes 311346240 | solution.py:241
  525.5 15.5 multiply_reduce_fusion.13
  605.8 15.5 multiply_reduce_fusion.13
  673.4 13.2 fusion.134
  691.5 52.5 %reduce-scatter.8.cloned.1.call-done = f32[2,256,1024]{2,1,0:T(8,128)} async-done(((f32[2,1024,1024]{2,1,0:T(8,128)}), f32[2,256,1024]{2,1,0:T(8,128)}) %reduce-scatter.8.cloned.1.call-update) | async-done | bytes 2097168 | tf_op jit(solution)/shard_map/reduce_scatter | solution.py:245
  746.8 71.6 %reduce-scatter.10.cloned.1.call-done = f32[2,256,1024]{2,1,0:T(8,128)} async-done(((f32[2,1024,1024]{2,1,0:T(8,128)}), f32[2,256,1024]{2,1,0:T(8,128)}) %reduce-scatter.10.cloned.1.call-update) | async-done | bytes 2097168 | tf_op jit(solution)/shard_map/reduce_scatter | solution.py:246
  832.3 12.2 convolution_dynamic-update-slice_fusion
  854.7 92.4 %reduce-scatter.14.cloned.1.call-done = f32[1024,1024]{1,0:T(8,128)} async-done(((f32[4096,1024]{1,0:T(8,128)}), f32[1024,1024]{1,0:T(8,128)}) %reduce-scatter.14.cloned.1.call-update) | async-done | bytes 4194320 | tf_op jit(solution)/shard_map/reduce_scatter | solution.py:276
  947.1 237.6 %reduce-scatter.12.cloned.1.call-done = f32[256,8192]{1,0:T(8,128)} async-done(((f32[1024,8192]{1,0:T(8,128)}), f32[256,8192]{1,0:T(8,128)}) %reduce-scatter.12.cloned.1.call-update) | async-done | bytes 8388624 | tf_op jit(solution)/shard_map/reduce_scatter | solution.py:261
  1198.2 38.0 %all-reduce.9 = (f32[256]{0:T(256)}, f32[256]{0:T(256)}, f32[256]{0:T(256)}, f32[1024]{0:T(1024)}, f32[256]{0:T(256)}, /*index=5*/f32[256]{0:T(256)}, f32[256]{0:T(256)}, f32[256]{0:T(256)}, f32[256]{0:T(256)}) all-reduce(f32[256]{0:T(256)S(1)} %dynamic-slice.1, f32[256]{0:T(256)S(1)} %dynamic-slice.3, ...), channel_id=1, replica_groups=mesh['dp'=8,'fsdp'=4] {'dp'}, use_global_device_ids=true, to_apply=%region_34.35 | all-reduce | flops 3072 | bytes 24576 | tf_op jit(solution)/shard_map/psum | solution.py:291
  1237.8 374.7 %all-reduce.14.cloned.1.call-done = (f32[256,8192]{1,0:T(8,128)}, f32[1024,1024]{1,0:T(8,128)}) async-done(((f32[256,8192]{1,0:T(8,128)}, f32[1024,1024]{1,0:T(8,128)}), (f32[256,8192]{1,0:T(8,128)}, f32[1024,1024]{1,0:T(8,128)})) %all-reduce.14.cloned.1.call-update) | async-done | bytes 12582928 | tf_op jit(solution)/shard_map/psum | solution.py:291
  (421 shorter events, 383.4 us)
Async XLA Ops:
  7.2 27.8 %all-gather.19.cloned.1.call-start = ((), (), s32[]{:S(2)}) async-start(), calls=%async_computation.5 | async-start | bytes 2621440 | tf_op jit(solution)/shard_map/all_gather | solution.py:170
  7.9 51.2 %all-gather.25.cloned.1.call-start = ((), (), s32[]{:S(2)}) async-start(), calls=%async_computation.8 | async-start | bytes 2621440 | tf_op jit(solution)/shard_map/all_gather | solution.py:169
  8.7 99.3 %all-gather.23.cloned.1.call-start = ((), (), s32[]{:S(2)}) async-start(), calls=%async_computation.7 | async-start | bytes 2621440 | tf_op jit(solution)/shard_map/all_gather | solution.py:168
  9.4 111.0 %all-gather.21.cloned.1.call-start = ((), (), s32[]{:S(2)}) async-start(), calls=%async_computation.6 | async-start | bytes 5242880 | tf_op jit(solution)/shard_map/all_gather | solution.py:188
  39.2 118.2 %all-gather.27.cloned.1.call-start = ((), (), s32[]{:S(2)}) async-start(), calls=%async_computation.9 | async-start | bytes 5242880 | tf_op jit(solution)/shard_map/all_gather | solution.py:187
  63.3 144.1 %all-gather.29.cloned.1.call-start = ((), (), s32[]{:S(2)}) async-start(), calls=%async_computation.10 | async-start | bytes 2621440 | tf_op jit(solution)/shard_map/all_gather | solution.py:171
  63.9 177.5 %all-gather.31.cloned.1.call-start = ((), (), s32[]{:S(2)}) async-start(), calls=%async_computation.11 | async-start | bytes 10485760 | tf_op jit(solution)/shard_map/all_gather | solution.py:172
  64.6 236.6 %all-gather.33.cloned.1.call-start = ((), (), s32[]{:S(2)}) async-start(), calls=%async_computation.12 | async-start | bytes 10485760 | tf_op jit(solution)/shard_map/all_gather | solution.py:173
  65.4 310.1 %all-gather.35.cloned.1.call-start = ((), (), s32[]{:S(2)}) async-start(), calls=%async_computation.13 | async-start | bytes 5242880 | tf_op jit(solution)/shard_map/all_gather | solution.py:214
  340.2 72.2 %all-gather.37.cloned.1.call-start = ((), (), s32[]{:S(2)}) async-start(), calls=%async_computation.14 | async-start | bytes 5242880 | tf_op jit(solution)/shard_map/all_gather | solution.py:213
  344.4 399.6 %reduce-scatter.8.cloned.1.call-start = ((), (), s32[]{:S(2)}) async-start(), calls=%async_computation.15 | async-start | bytes 10485760 | tf_op jit(solution)/shard_map/reduce_scatter | solution.py:245
  672.2 146.2 %reduce-scatter.10.cloned.1.call-start = ((), (), s32[]{:S(2)}) async-start(), calls=%async_computation.16 | async-start | bytes 10485760 | tf_op jit(solution)/shard_map/reduce_scatter | solution.py:246
  672.8 274.4 %reduce-scatter.14.cloned.1.call-start = ((), (), s32[]{:S(2)}) async-start(), calls=%async_computation.18 | async-start | bytes 20971520 | tf_op jit(solution)/shard_map/reduce_scatter | solution.py:276
  686.5 498.2 %reduce-scatter.12.cloned.1.call-start = ((), (), s32[]{:S(2)}) async-start(), calls=%async_computation.17 | async-start | bytes 41943040 | tf_op jit(solution)/shard_map/reduce_scatter | solution.py:261
  844.5 391.7 %reduce-scatter.16.cloned.1.call-start = ((), (), s32[]{:S(2)}) async-start(), calls=%async_computation.19 | async-start | bytes 655360
  853.5 331.3 %copy-start.80 = (u32[32]{0:T(128)S(1)}, u32[32]{0:T(128)}, u32[]{:S(2)}) copy-start(u32[32]{0:T(128)} %constant.161) | copy-start | bytes 388
  853.5 333.4 %copy-start.43 = (f32[1024]{0:T(1024)S(1)}, f32[1024]{0:T(1024)}, u32[]{:S(2)}) copy-start(f32[1024]{0:T(1024)} %get-tuple-element.296) | copy-start | bytes 12292
  853.5 333.5 %copy-start.44 = (f32[1024]{0:T(1024)S(1)}, f32[1024]{0:T(1024)}, u32[]{:S(2)}) copy-start(f32[1024]{0:T(1024)} %get-tuple-element.197) | copy-start | bytes 12292
  853.5 333.5 %copy-start.45 = (f32[1024]{0:T(1024)S(1)}, f32[1024]{0:T(1024)}, u32[]{:S(2)}) copy-start(f32[1024]{0:T(1024)} %get-tuple-element.262) | copy-start | bytes 12292
  853.5 333.5 %copy-start.46 = (f32[1024]{0:T(1024)S(1)}, f32[1024]{0:T(1024)}, u32[]{:S(2)}) copy-start(f32[1024]{0:T(1024)} %get-tuple-element.266) | copy-start | bytes 12292
  853.5 333.5 %copy-start.48 = (f32[4096]{0:T(1024)S(1)}, f32[4096]{0:T(1024)}, u32[]{:S(2)}) copy-start(f32[4096]{0:T(1024)} %get-tuple-element.264) | copy-start | bytes 49156
  853.5 333.5 %copy-start.56 = (f32[1024]{0:T(1024)S(1)}, f32[1024]{0:T(1024)}, u32[]{:S(2)}) copy-start(f32[1024]{0:T(1024)} %get-tuple-element.199) | copy-start | bytes 12292
  853.5 333.5 %copy-start.57 = (f32[1024]{0:T(1024)S(1)}, f32[1024]{0:T(1024)}, u32[]{:S(2)}) copy-start(f32[1024]{0:T(1024)} %get-tuple-element.201) | copy-start | bytes 12292
  854.7 757.8 %all-reduce.14.cloned.1.call-start = ((), (), s32[]{:S(2)}) async-start(), calls=%async_computation.20 | async-start | bytes 25165824 | tf_op jit(solution)/shard_map/psum | solution.py:291
  (99 other events, 2435.5 us)
Sparse Core Ops, SparseCore 0:
  9.6 25.3 all-gather.18
  36.6 22.4 all-gather.24
  60.6 22.6 all-gather.22
  85.3 35.0 all-gather.20
  122.4 35.0 all-gather.26
  158.8 22.5 all-gather.28
  183.0 58.2 all-gather.30
  242.9 58.2 all-gather.32
  340.3 35.0 all-gather.34
  377.4 34.9 all-gather.36
  672.3 71.7 reduce-scatter.7
  746.7 71.6 reduce-scatter.9
  821.0 126.1 reduce-scatter.13
  949.8 234.9 reduce-scatter.11
  1187.8 21.6 reduce-scatter.15
  1213.7 398.8 all-reduce.13
where the time goes:
time: 1630 us
  waiting for transfers between devices  1060 us (65%)
  matrix products  302 us (19%)
  local copies, waits for them, and re-layouts  106 us (7%)
  blocking collectives  95.8 us (6%)
  other arithmetic  45.8 us (3%)
  between operations  17.1 us (1%)
    psum x1, waiting for transfers between devices, per_device(): lax.psum((wide_shard, down_shard, small_shards[0], small_shards[1], small...  375 us
    reduce_scatter x1, waiting for transfers between devices, per_device(): lax.psum_scatter(jnp.concatenate([outer_sum(rounded, query_delta), outer_...  238 us
    reduce_scatter x1, waiting for transfers between devices, per_device(): lax.psum_scatter(outer_sum(activated, down_delta), 'fsdp', scatter_dimens...  92.4 us
    dot_general x11, matrix products, project(): return jnp.dot(rows_in, matrix, preferred_element_type=jnp.float32)  88.2 us
    all_gather x2, waiting for transfers between devices, per_device(): lax.all_gather(key_rows, 'fsdp', axis=1, tiled=True)  74 us
    reduce_scatter x1, waiting for transfers between devices, per_device(): lax.psum_scatter(value_part, 'fsdp', scatter_dimension=1, tiled=True)  71.6 us
    all_gather x1, waiting for transfers between devices, per_device(): lax.all_gather(down_weight, 'fsdp', axis=0, tiled=True)  59.9 us
    reduce_scatter x1, waiting for transfers between devices, per_device(): lax.psum_scatter(key_part, 'fsdp', scatter_dimension=1, tiled=True)  52.5 us
  transfers between devices with their start and end apart: 16, of which 13 were waited for; matrix products, arithmetic and copies ran while one was open for 9% of the time, Pallas kernels for 0%

commit v1 on v0

v1 whole, which is shorter than its diff:
```python
import functools
import math

import jax
import jax.numpy as jnp
from jax import lax
from jax.experimental import pallas as pl
from jax.experimental.pallas import tpu as pltpu
from jax.sharding import PartitionSpec as P

D = 1024
HEADS = 16
HEAD_DIM = 64
GROUP = 256
GROUP_HEADS = GROUP // HEAD_DIM
F32 = jnp.float32
BF16 = jnp.bfloat16
ROWS_ROWS = (((0,), (0,)), ((), ()))
COLS_COLS = (((1,), (1,)), ((), ()))
KERNEL = pltpu.CompilerParams(vmem_limit_bytes=50 * 2**20)
ANY = pl.BlockSpec(memory_space=pl.ANY)


def sinusoid(timestep):
    halves = D // 2
    frequency = jnp.exp(jnp.arange(halves, dtype=F32) * (-math.log(10000.0) / halves))
    angles = timestep.astype(F32)[:, None] * frequency[None, :]
    return jnp.concatenate([jnp.sin(angles), jnp.cos(angles)], axis=1)


def head_mask(head):
    return lax.broadcasted_iota(jnp.int32, (1, GROUP), 1) // HEAD_DIM == head


def cost(flops, nbytes):
    return pl.CostEstimate(flops=flops, bytes_accessed=nbytes, transcendentals=0)


def attend_kernel(tile, q_ref, k1_ref, k2_ref, v1_ref, v2_ref, out_ref, lse_ref):
    keys = jnp.concatenate([k1_ref[...], k2_ref[...]], axis=0)
    values_t = jnp.concatenate([v1_ref[...], v2_ref[...]], axis=0).T
    for start in range(0, q_ref.shape[0], tile):
        rows = pl.ds(start, tile)
        queries = q_ref[rows, :] * jnp.asarray(HEAD_DIM**-0.5, BF16)
        outs = []
        for head in range(GROUP_HEADS):
            masked = jnp.where(head_mask(head), queries, jnp.zeros_like(queries))
            scores = lax.dot_general(keys, masked, COLS_COLS, preferred_element_type=F32)
            peak = jnp.max(scores, axis=0, keepdims=True)
            exponent = jnp.exp(scores - peak)
            total = jnp.sum(exponent, axis=0, keepdims=True)
            attention = (exponent * (1.0 / total)).astype(BF16)
            lse_ref[0, head : head + 1, rows] = peak + jnp.log(total)
            own = values_t[head * HEAD_DIM : (head + 1) * HEAD_DIM, :]
            outs.append(jnp.dot(own, attention, preferred_element_type=F32))
        out_ref[rows, :] = jnp.concatenate(outs, axis=0).astype(BF16).T


def group_columns(rows, first=0):
    return pl.BlockSpec((rows, GROUP), lambda g: (0, first + g))


def attend(queries, k1, k2, v1, v2):
    tokens, width = queries.shape
    keys = k1.shape[0]
    groups = width // GROUP
    return pl.pallas_call(
        functools.partial(attend_kernel, min(512, tokens)),
        grid=(groups,),
        in_specs=[group_columns(tokens)] + [group_columns(keys)] * 4,
        out_specs=[
            group_columns(tokens),
            pl.BlockSpec((1, GROUP_HEADS, tokens), lambda g: (g, 0, 0)),
        ],
        out_shape=[
            jax.ShapeDtypeStruct((tokens, width), BF16),
            jax.ShapeDtypeStruct((groups, GROUP_HEADS, tokens), F32),
        ],
        compiler_params=KERNEL,
        cost_estimate=cost(20 * 10**9, 6 * 2**20),
        name="attend",
    )(queries, k1, k2, v1, v2)


def attend_back_kernel(
    tile, q_ref, k1_ref, k2_ref, v1_ref, v2_ref, lse_ref, grad_ref,
    dq_ref, dk1_ref, dk2_ref, dv1_ref, dv2_ref, p_all, ds_all, dk_sum, dv_sum,
):
    half = k1_ref.shape[0]
    keys = jnp.concatenate([k1_ref[...], k2_ref[...]], axis=0)
    values = jnp.concatenate([v1_ref[...], v2_ref[...]], axis=0)
    keys_t = keys.T
    for start in range(0, q_ref.shape[0], tile):
        rows = pl.ds(start, tile)
        queries = q_ref[rows, :] * jnp.asarray(HEAD_DIM**-0.5, BF16)
        grads = grad_ref[rows, :]
        query_parts, grad_parts, dq_parts = [], [], []
        for head in range(GROUP_HEADS):
            query_one = jnp.where(head_mask(head), queries, jnp.zeros_like(queries))
            grad_one = jnp.where(head_mask(head), grads, jnp.zeros_like(grads))
            scores = lax.dot_general(keys, query_one, COLS_COLS, preferred_element_type=F32)
            attention = jnp.exp(scores - lse_ref[0, head : head + 1, rows])
            prob_grad = lax.dot_general(values, grad_one, COLS_COLS, preferred_element_type=F32)
            weighted = jnp.sum(attention * prob_grad, axis=0, keepdims=True)
            score_grad = (attention * (prob_grad - weighted)).astype(BF16)
            place = slice(head * tile, (head + 1) * tile)
            p_all[:, place] = attention.astype(BF16)
            ds_all[:, place] = score_grad
            own = keys_t[head * HEAD_DIM : (head + 1) * HEAD_DIM, :]
            dq_parts.append(jnp.dot(own, score_grad, preferred_element_type=F32))
            query_parts.append(query_one)
            grad_parts.append(grad_one)
        dv_tile = jnp.dot(p_all[...], jnp.concatenate(grad_parts, axis=0), preferred_element_type=F32)
        dk_tile = jnp.dot(ds_all[...], jnp.concatenate(query_parts, axis=0), preferred_element_type=F32)
        if start == 0:
            dv_sum[...] = dv_tile
            dk_sum[...] = dk_tile
        else:
            dv_sum[...] += dv_tile
            dk_sum[...] += dk_tile
        dq_ref[rows, :] = (jnp.concatenate(dq_parts, axis=0) * HEAD_DIM**-0.5).astype(BF16).T
    dk1_ref[...] = dk_sum[:half, :]
    dk2_ref[...] = dk_sum[half:, :].astype(BF16)
    dv1_ref[...] = dv_sum[:half, :]
    dv2_ref[...] = dv_sum[half:, :].astype(BF16)


def attend_back(queries, k1, k2, v1, v2, lse, mixed_grad, first, groups):
    tokens = queries.shape[0]
    keys = k1.shape[0]
    tile = min(512, tokens)
    width = groups * GROUP
    lse_spec = pl.BlockSpec((1, GROUP_HEADS, tokens), lambda g: (first + g, 0, 0))
    return pl.pallas_call(
        functools.partial(attend_back_kernel, tile),
        grid=(groups,),
        in_specs=[group_columns(tokens, first)]
        + [group_columns(keys, first)] * 4
        + [lse_spec, group_columns(tokens, first)],
        out_specs=[group_columns(tokens)] + [group_columns(keys)] * 4,
        out_shape=[
            jax.ShapeDtypeStruct((tokens, width), BF16),
            jax.ShapeDtypeStruct((keys, width), F32),
            jax.ShapeDtypeStruct((keys, width), BF16),
            jax.ShapeDtypeStruct((keys, width), F32),
            jax.ShapeDtypeStruct((keys, width), BF16),
        ],
        scratch_shapes=[
            pltpu.VMEM((2 * keys, GROUP_HEADS * tile), BF16),
            pltpu.VMEM((2 * keys, GROUP_HEADS * tile), BF16),
            pltpu.VMEM((2 * keys, GROUP), F32),
            pltpu.VMEM((2 * keys, GROUP), F32),
        ],
        compiler_params=KERNEL,
        cost_estimate=cost(8 * 10**9 * groups, 4 * 2**20 * groups),
        name="attend_back",
    )(queries, k1, k2, v1, v2, lse, mixed_grad)


def gelu_and_slope(upward):
    size = jnp.abs(upward) * (2.0**-0.5)
    bell = jnp.exp(-0.5 * (upward * upward))
    t = 1.0 / (1.0 + 0.3275911 * size)
    series = t * (
        0.254829592
        + t * (-0.284496736 + t * (1.421413741 + t * (-1.453152027 + t * 1.061405429)))
    )
    tail = 0.5 * series * bell
    cdf = jnp.where(upward >= 0, 1.0 - tail, tail)
    return upward * cdf, cdf + upward * (bell * (2 * math.pi) ** -0.5)


def up_kernel(rows_ref, weight_ref, bias_ref, active_ref, slope_ref):
    upward = jnp.dot(rows_ref[...], weight_ref[...], preferred_element_type=F32)
    active, slope = gelu_and_slope(upward + bias_ref[...].astype(F32))
    active_ref[...] = active.astype(BF16)
    slope_ref[...] = slope.astype(BF16)


def up_project(rows_in, weight, bias):
    tokens, width = rows_in.shape
    columns = weight.shape[1]
    step = 512
    by_column = lambda rows: pl.BlockSpec((rows, step), lambda j: (0, j))
    return pl.pallas_call(
        up_kernel,
        grid=(columns // step,),
        in_specs=[pl.BlockSpec((tokens, width), lambda j: (0, 0)), by_column(width), by_column(1)],
        out_specs=[by_column(tokens)] * 2,
        out_shape=[jax.ShapeDtypeStruct((tokens, columns), BF16)] * 2,
        compiler_params=KERNEL,
        cost_estimate=cost(15 * 10**9, 17 * 2**20),
        name="up_project",
    )(rows_in, weight, bias.reshape(1, columns))


def place_kernel(place_ref, *refs):
    pieces, out_ref = refs[:-1], refs[-1]
    for i, piece in enumerate(pieces):
        start = pl.multiple_of(place_ref[i], 16)
        out_ref[pl.ds(start, piece.shape[0]), :] = piece[...]


def place(places, pieces):
    rows = sum(piece.shape[0] for piece in pieces)
    columns = pieces[0].shape[1]
    step = min(columns, 2**20 // rows)
    by_column = lambda n: pl.BlockSpec((n, step), lambda j, at: (0, j))
    return pl.pallas_call(
        place_kernel,
        grid_spec=pltpu.PrefetchScalarGridSpec(
            num_scalar_prefetch=1,
            grid=(columns // step,),
            in_specs=[by_column(piece.shape[0]) for piece in pieces],
            out_specs=by_column(rows),
        ),
        out_shape=jax.ShapeDtypeStruct((rows, columns), pieces[0].dtype),
        compiler_params=KERNEL,
        cost_estimate=cost(0, 4 * rows * columns),
        name="place",
    )(places, *pieces)


def grad_kernel(where_ref, left_ref, right_ref, far_left_ref, far_right_ref, out_ref):
    near = lax.dot_general(left_ref[...], right_ref[...], ROWS_ROWS, preferred_element_type=F32)
    far = lax.dot_general(far_left_ref[...], far_right_ref[...], ROWS_ROWS, preferred_element_type=F32)
    out_ref[...] = (near + far).astype(BF16)


def grad_rows(left, right, far_left, far_right, near_row, far_row, rows, first_column=0, columns=None):
    tokens = right.shape[0]
    columns = right.shape[1] if columns is None else columns
    step = 256
    row_steps = rows // step
    at_column = first_column // D
    where = jnp.stack([near_row // step, far_row // step]).astype(jnp.int32)
    return pl.pallas_call(
        grad_kernel,
        grid_spec=pltpu.PrefetchScalarGridSpec(
            num_scalar_prefetch=1,
            grid=(columns // D, row_steps),
            in_specs=[
                pl.BlockSpec((tokens, step), lambda j, i, at: (0, at[0] + i)),
                pl.BlockSpec((tokens, D), lambda j, i, at: (0, at_column + j)),
                pl.BlockSpec((tokens, step), lambda j, i, at: (0, at[1] + i)),
                pl.BlockSpec((tokens, D), lambda j, i, at: (0, at_column + j)),
            ],
            out_specs=pl.BlockSpec((step, D), lambda j, i, at: (j * row_steps + i, 0)),
        ),
        out_shape=jax.ShapeDtypeStruct((rows * columns // D, D), BF16),
        compiler_params=KERNEL,
        cost_estimate=cost(4 * tokens * rows * columns, 2 * (rows * columns + 2 * tokens * columns)),
        name="grad_rows",
    )(where, left, right, far_left, far_right)


def project(rows_in, matrix):
    return jnp.dot(rows_in, matrix, preferred_element_type=F32)


def project_back(rows_in, matrix):
    return lax.dot_general(rows_in, matrix, COLS_COLS, preferred_element_type=F32)


def normalise(residual):
    centered = residual - jnp.mean(residual, axis=-1, keepdims=True)
    scale = lax.rsqrt(jnp.mean(centered * centered, axis=-1, keepdims=True) + 1e-05)
    return centered * scale, scale


def normalise_back(unit, scale, gain, grad_rows_in):
    scaled = grad_rows_in * gain
    inner = jnp.mean(scaled * unit, axis=-1, keepdims=True)
    return scale * (scaled - jnp.mean(scaled, axis=-1, keepdims=True) - unit * inner)


def column_sum(rows_in):
    return jnp.sum(rows_in.astype(F32), axis=0)


def after(value, *others):
    return lax.optimization_barrier((value, *others))[0]


def dynamic_rows(array, start, rows):
    return lax.dynamic_slice_in_dim(array, start, rows, axis=0)


def per_device(
    n_dp,
    inputs,
    timestep,
    bucket_count,
    upstream,
    query_weight,
    key_weight,
    value_weight,
    output_weight,
    up_weight,
    down_weight,
    *vectors,
):
    device = lax.axis_index("fsdp")
    chip, core = device // 2, device % 2
    bucket = lax.axis_index("dp")

    def swap(value, axis, bit):
        size = 4 if axis == "fsdp" else n_dp
        return lax.ppermute(value, axis, [(i, i ^ bit) for i in range(size)])

    def swap_core(value):
        return swap(value, "fsdp", 1)

    def swap_chip(value):
        return swap(value, "fsdp", 2)

    def split_pair(pair):
        mine = lax.dynamic_index_in_dim(pair, chip, keepdims=False)
        theirs = lax.dynamic_index_in_dim(pair, 1 - chip, keepdims=False)
        return mine, theirs

    def from_sequence(mine, received):
        order = lambda first, second: jnp.stack([first, second])
        return jnp.where(chip == 0, order(mine, received), order(received, mine))

    def fetch(shard, bit, *before):
        rows = shard.shape[0]
        side = (bucket // bit) % 2
        return swap_chip(after(dynamic_rows(shard, side * (rows // 2), rows // 2), *before))

    def gather(shard, first, bit):
        rows = shard.shape[0]
        side = (bucket // bit) % 2
        second = swap(first, "dp", bit)
        pieces = [shard, first, second]
        pieces = pieces + [swap_core(piece) for piece in pieces]
        far = device ^ 2
        places = []
        for flip in (0, 1):
            places += [
                (device ^ flip) * rows,
                (far ^ flip) * rows + side * (rows // 2),
                (far ^ flip) * rows + (1 - side) * (rows // 2),
            ]
        return place(jnp.stack(places).astype(jnp.int32), pieces)

    y_bit, z_bit = 1, min(2, n_dp // 2)
    tokens_mine, tokens_theirs = split_pair(inputs)
    tokens = jnp.concatenate([tokens_mine, swap_chip(tokens_theirs)], axis=0)
    qkv_weight = jnp.concatenate([query_weight, key_weight, value_weight], axis=1)
    qkv_first = fetch(qkv_weight, y_bit)
    qkv_full = gather(qkv_weight, qkv_first, y_bit)
    small = jnp.concatenate(vectors)
    pair = jnp.stack([small, swap_chip(small)])
    quad = jnp.stack([pair, swap_core(pair)])
    shares = [quad[i & 1, i >> 1] for i in range(4)]
    ordered = [
        jnp.where(device == 0, shares[i], jnp.where(device == 1, shares[i ^ 1], jnp.where(device == 2, shares[i ^ 2], shares[i ^ 3])))
        for i in range(4)
    ]
    full, at = [], 0
    for vector in vectors:
        n = vector.shape[0]
        full.append(jnp.concatenate([share[at : at + n] for share in ordered]).astype(F32))
        at += n
    query_bias, value_bias, output_bias, up_bias, down_bias, gain1, shift1, gain2, shift2 = full
    output_first = fetch(output_weight, z_bit, tokens)
    up_first = fetch(up_weight, z_bit, tokens)
    down_first = fetch(down_weight, y_bit, qkv_first)
    output_full = gather(output_weight, output_first, z_bit)
    up_full = gather(up_weight, up_first, z_bit)
    down_full = gather(down_weight, down_first, y_bit)
    upstream_mine, upstream_theirs = split_pair(upstream)
    upstream_theirs = after(upstream_theirs, output_first)
    cotangent_rows = jnp.concatenate([upstream_mine, swap_chip(upstream_theirs)], axis=0)

    embedding = lax.dynamic_index_in_dim(sinusoid(timestep), chip, keepdims=False)
    hidden = tokens.astype(F32) + embedding[None, :]
    rounded = hidden.astype(BF16)
    key_rows = project(rounded, qkv_full[:, D : 2 * D]).astype(BF16)
    values = (project(rounded, qkv_full[:, 2 * D :]) + value_bias).astype(BF16)
    far_keys, far_values = swap_core(key_rows), swap_core(values)
    queries = (project(rounded, qkv_full[:, :D]) + query_bias).astype(BF16)
    mixed, lse = attend(queries, key_rows, far_keys, values, far_values)

    unit1, scale1 = normalise(hidden + (project(mixed, output_full) + output_bias))
    first_norm = unit1 * gain1 + shift1
    first_low = first_norm.astype(BF16)
    activated, slope = up_project(first_low, up_full, up_bias)
    unit2, scale2 = normalise(first_norm + (project(activated, down_full) + down_bias))
    activations = (unit2 * gain2 + shift2).astype(BF16)
    split = inputs.shape[1]

    live = chip < bucket_count[bucket]
    seq_weight = live.astype(F32) * (2 * n_dp / jnp.sum(bucket_count).astype(F32))
    cotangent = cotangent_rows.astype(F32) * seq_weight
    gain2_part = column_sum(cotangent * unit2)
    shift2_part = column_sum(cotangent)
    second_grad = normalise_back(unit2, scale2, gain2, cotangent)
    down_delta = second_grad.astype(BF16)
    down_bias_part = column_sum(down_delta)

    low_bits = [bit for bit in (1, 2) if bit < n_dp]
    high_bits = [1 << i for i in range(2, n_dp.bit_length()) if 1 << i < n_dp]
    sides = [(bucket // bit) % 2 for bit in low_bits]

    def both_cores(left, right):
        rows = left.shape[1] // 4
        away = jnp.concatenate(
            [
                lax.dynamic_slice_in_dim(left, (2 * i + 1 - core) * rows, rows, axis=1)
                for i in (0, 1)
            ],
            axis=1,
        )
        return left, right, swap_core(away), swap_core(right)

    def grad_part(sides_of, to_chip, rows, first_row=0, **columns):
        whole = sides_of[0].shape[1] // 4
        near, far = (2 * to_chip + core) * whole + first_row, to_chip * whole + first_row
        return grad_rows(*sides_of, near, far, rows, **columns)

    def fold(mine, received, level):
        half = mine.shape[0] // 2
        side = sides[level]
        add = lambda start: (
            dynamic_rows(mine, start, half).astype(F32) + dynamic_rows(received, start, half).astype(F32)
        ).astype(BF16)
        return add(side * half), add((1 - side) * half)

    def finish(mine, received):
        for level in range(1, len(low_bits)):
            mine, away = fold(mine, received, level)
            received = swap(away, "dp", low_bits[level])
        total = (mine.astype(F32) + received.astype(F32)).astype(BF16)
        for bit in high_bits:
            total = (total.astype(F32) + swap(total, "dp", bit).astype(F32)).astype(BF16)
        for bit, side in reversed(list(zip(low_bits, sides))):
            other = swap(total, "dp", bit)
            total = jnp.where(side == 0, jnp.stack([total, other]), jnp.stack([other, total])).reshape(-1, total.shape[1])
        return total.astype(F32)

    class Chunk:
        def __init__(self, make):
            self.sent = make(1 - chip)
            self.make = make
            self.received = swap_chip(self.sent)

        def second(self):
            self.mine, self.away = fold(self.make(chip), self.received, 0)
            self.arrived = swap(self.away, "dp", low_bits[0])
            return self.away

        def result(self):
            return finish(self.mine, self.arrived)

    down_sides = both_cores(activated, down_delta)
    half_rows = activated.shape[1] // 8
    up_grad_in = project_back(down_delta, down_full)
    up_delta = (up_grad_in * slope.astype(F32)).astype(BF16)
    up_bias_part = column_sum(up_delta)
    down1 = Chunk(lambda to: grad_part(down_sides, to, half_rows))
    down2 = Chunk(lambda to: grad_part(down_sides, to, half_rows, half_rows))
    up_sides = both_cores(first_low, up_delta)
    up_delta = after(up_delta, down1.sent, down2.sent)
    up_columns = up_delta.shape[1] // 2
    up1 = Chunk(lambda to: grad_part(up_sides, to, D // 4, first_column=0, columns=up_columns))
    up2 = Chunk(lambda to: grad_part(up_sides, to, D // 4, first_column=up_columns, columns=up_columns))
    first_grad = second_grad + project_back(up_delta, up_full)
    gain1_part = column_sum(first_grad * unit1)
    shift1_part = column_sum(first_grad)
    first_input_grad = normalise_back(unit1, scale1, gain1, first_grad)
    out_delta = first_input_grad.astype(BF16)
    output_bias_part = column_sum(out_delta)
    mixed_grad = project_back(out_delta, output_full).astype(BF16)
    output_sides = both_cores(mixed, out_delta)
    output1 = Chunk(lambda to: grad_part(output_sides, to, D // 4))
    mixed_grad = after(mixed_grad, up1.sent, up2.sent, down1.second())
    activations_away = after(activations[split:], output1.sent)

    qkv_forward = (queries, key_rows, far_keys, values, far_values, lse)
    groups = D // GROUP // 2
    first_half = attend_back(*qkv_forward, mixed_grad, 0, groups)
    mixed_grad = after(mixed_grad, first_half[0], down2.second(), down1.arrived, output1.sent)
    second_half = attend_back(*qkv_forward, mixed_grad, groups, groups)
    query_delta, dk_mine, dk_far, dv_mine, dv_far = [
        jnp.concatenate(halves, axis=1) for halves in zip(first_half, second_half)
    ]
    key_delta = (dk_mine + swap_core(dk_far).astype(F32)).astype(BF16)
    value_delta = (dv_mine + swap_core(dv_far).astype(F32)).astype(BF16)
    query_bias_part = column_sum(query_delta)
    value_bias_part = column_sum(value_delta)
    deltas = jnp.concatenate([query_delta, key_delta, value_delta], axis=1)
    qkv_sides = both_cores(rounded, deltas)
    qkv1 = Chunk(lambda to: grad_part(qkv_sides, to, D // 4, first_column=0, columns=2 * D))
    qkv2 = Chunk(lambda to: grad_part(qkv_sides, to, D // 4, first_column=2 * D, columns=D))
    for chunk in (up1, up2, output1, qkv1, qkv2):
        chunk.second()
    deltas = after(deltas, qkv1.sent, qkv2.sent)
    input_grad = first_input_grad + project_back(deltas, qkv_full)
    received = swap_chip(input_grad[split:].astype(BF16)).astype(F32)
    input_gradient = from_sequence(input_grad[:split], received)
    activations_out = from_sequence(activations[:split], swap_chip(activations_away))

    time_sum = column_sum(input_grad)
    time_sum = time_sum + swap_core(time_sum)
    time_both = from_sequence(time_sum, swap_chip(time_sum))
    time_gradient = lax.dynamic_slice_in_dim(time_both, device * (D // 4), D // 4, axis=1)

    parts = [
        query_bias_part, value_bias_part, output_bias_part, up_bias_part, down_bias_part,
        gain1_part, shift1_part, gain2_part, shift2_part,
    ]
    packed = jnp.concatenate(parts).reshape(-1, 128)
    for axis, size in (("fsdp", 4), ("dp", n_dp)):
        bit = 1
        while bit < size:
            packed = packed + swap(packed, axis, bit)
            bit *= 2
    packed = packed.reshape(-1)
    vector_grads, at = [], 0
    for part in parts:
        n = part.shape[0]
        vector_grads.append(lax.dynamic_slice_in_dim(packed[at : at + n], device * (n // 4), n // 4))
        at += n

    qkv_total = qkv1.result()
    up_total = jnp.concatenate([up1.result(), up2.result()]).reshape(-1, D // 4, D)
    return (
        activations_out,
        input_gradient,
        time_gradient,
        qkv_total[: D // 4],
        qkv_total[D // 4 :],
        qkv2.result(),
        output1.result(),
        up_total.transpose(1, 0, 2).reshape(D // 4, -1),
        jnp.concatenate([down1.result(), down2.result()], axis=0),
        *vector_grads,
    )


def solution(mesh):
    rows, wide, flat = P("dp", "fsdp", None), P("fsdp", None), P("fsdp")
    return jax.shard_map(
        functools.partial(per_device, mesh.shape["dp"]),
        mesh=mesh,
        in_specs=(rows, P("dp"), P(), rows) + (wide,) * 6 + (flat,) * 9,
        out_specs=(rows, rows, P("dp", "fsdp")) + (wide,) * 6 + (flat,) * 9,
        check_vma=False,
    )
```

time: 1630 us -> 575 us (0.35)
  waiting for transfers between devices: 1060 us -> 238 us
  matrix products: 302 us -> 48.5 us
  Pallas kernels: 0 us -> 131 us
  blocking collectives: 95.8 us -> 0 us
  starting transfers between devices: 0.64 us -> 63.2 us
  local copies, waits for them, and re-layouts: 106 us -> 43.5 us
    reduce_scatter x4 -> x0, waiting for transfers between devices: 454 us -> none  [the longest x1 238 us: per_device(): lax.psum_scatter(jnp.concatenate([outer_sum(rounded, query_delta), outer_...]
    psum x1 -> x0, waiting for transfers between devices: 375 us -> none  [per_device(): lax.psum((wide_shard, down_shard, small_shards[0], small_shards[1], small...]
    ppermute x0 -> x87, waiting for transfers between devices: none -> 238 us  [swap(): return lax.ppermute(value, axis, [(i, i ^ bit) for i in range(size)])]
    dot_general x39 -> x9, matrix products: 281 us -> 48.5 us  [the longest x4 27.1 us: project_back(): lax.dot_general(rows_in, matrix, COLS_COLS, preferred_element_type=F32)]
    all_gather x10 -> x0, waiting for transfers between devices: 228 us -> none  [the longest x2 74 us: per_device(): lax.all_gather(key_rows, 'fsdp', axis=1, tiled=True)]
    pallas_call x0 -> x22, Pallas kernels: none -> 131 us  [the longest x14 45.7 us: grad_rows(): pl.pallas_call(grad_kernel, grid_spec=pltpu.PrefetchScalarGridSpec(num_sc...]
    ppermute x0 -> x87, starting transfers between devices: none -> 63.2 us  [swap(): return lax.ppermute(value, axis, [(i, i ^ bit) for i in range(size)])]
    all_gather x9 -> x0, blocking collectives: 47.2 us -> none  [the longest x1 5.97 us: per_device(): lax.all_gather(value_bias, 'fsdp', axis=0, tiled=True)]
  transfers between devices with their start and end apart: 16 -> 87, of which waited for: 13 -> 38; matrix products, arithmetic and copies ran while one was open for 9% -> 21% of each run, Pallas kernels for 0% -> 23%
where the time goes in v1:
time: 575 us; the launch traced here: 567 us
  waiting for transfers between devices  238 us (41%)
  Pallas kernels  131 us (23%)
  starting transfers between devices  63.2 us (11%)
  matrix products  48.5 us (8%)
  local copies, waits for them, and re-layouts  43.5 us (8%)
  other arithmetic  38.2 us (7%)
    ppermute x87, waiting for transfers between devices, swap(): return lax.ppermute(value, axis, [(i, i ^ bit) for i in range(size)])  238 us
    ppermute x87, starting transfers between devices, swap(): return lax.ppermute(value, axis, [(i, i ^ bit) for i in range(size)])  63.2 us
    pallas_call x14, Pallas kernels, grad_rows(): pl.pallas_call(grad_kernel, grid_spec=pltpu.PrefetchScalarGridSpec(num_sc...  45.7 us
    pallas_call x2, Pallas kernels, attend_back(): pl.pallas_call(functools.partial(attend_back_kernel, tile), grid=(groups,...  30.9 us
    dot_general x4, matrix products, project_back(): lax.dot_general(rows_in, matrix, COLS_COLS, preferred_element_type=F32)  27.1 us
    dot_general x5, matrix products, project(): return jnp.dot(rows_in, matrix, preferred_element_type=F32)  21.4 us
    pallas_call x4, Pallas kernels, place(): pl.pallas_call(place_kernel, grid_spec=pltpu.PrefetchScalarGridSpec(num_s...  21.3 us
    pallas_call x1, Pallas kernels, attend(): pl.pallas_call(functools.partial(attend_kernel, min(512, tokens)), grid=(...  18.3 us
  transfers between devices with their start and end apart: 87, of which 38 were waited for; matrix products, arithmetic and copies ran while one was open for 21% of the time, Pallas kernels for 23%

profile of v1, /device:TPU:0, one launch (start us, length us, event | category | flops | bytes accessed | tf_op | source)
XLA Modules:
  0.0 566.6 jit_solution(12595293661716377476)
XLA Ops:
  27.9 15.9 %collective-permute-done.1.refs_1_ = bf16[128,3072]{1,0:T(8,128)(2,1)S(1)} collective-permute-done((bf16[128,3072]{1,0:T(8,128)(2,1)}, bf16[128,3072]{1,0:T(8,128)(2,1)S(1)}, u32[]{:S(2)}, u32[]{:S(2)}) %collective-permute-start.1) | collective-permute-done | bytes 786464 | tf_op jit(solution)/shard_map/ppermute | solution.py:309
  46.2 15.7 %collective-permute-done.2.refs_2_ = bf16[128,3072]{1,0:T(8,128)(2,1)S(1)} collective-permute-done((bf16[128,3072]{1,0:T(8,128)(2,1)S(1)}, bf16[128,3072]{1,0:T(8,128)(2,1)S(1)}, u32[]{:S(2)}, u32[]{:S(2)}) %collective-permute-start.2) | collective-permute-done | bytes 786464 | tf_op jit(solution)/shard_map/ppermute | solution.py:309
  64.0 10.7 %collective-permute-done.10.refs_1_ = bf16[128,1024]{1,0:T(8,128)(2,1)S(1)} collective-permute-done((bf16[128,1024]{1,0:T(8,128)(2,1)}, bf16[128,1024]{1,0:T(8,128)(2,1)S(1)}, u32[]{:S(2)}, u32[]{:S(2)}) %collective-permute-start.10) | collective-permute-done | bytes 262176 | tf_op jit(solution)/shard_map/ppermute | solution.py:309
  106.6 18.3 %attend.1 = (bf16[512,1024]{1,0:T(8,128)(2,1)S(1)}, f32[4,4,512]{2,1,0:T(4,128)S(1)}) custom-call(bf16[512,1024]{1,0:T(8,128)(2,1)S(1)} %add_convert_fusion.2.q_ref, bf16[512,1024]{1,0:T(8,128)(2,1)S(1)} %fusion.17.k1_ref, bf16[512,1024]{1,0:T(8,128)(2,1)} %collective-permute-done.8.k2_ref, bf16[512,1024]{1,0:T(8,128)(2,1)} %add_convert_fusion.1.v1_ref, ...), custom_call_target="tpu_custom_call" | custom-call | flops 20000000000 | bytes 6291456 | tf_op jit(solution)/shard_map/attend/pallas_call | solution.py:67
  131.5 6.8 %place.6.weight_ref = bf16[1024,4096]{1,0:T(8,128)(2,1)} custom-call(s32[6]{0:T(128)S(1)} %stack.388.place_ref, bf16[256,4096]{1,0:T(8,128)(2,1)} %refs_0_.4, bf16[128,4096]{1,0:T(8,128)(2,1)S(1)} %collective-permute-done.15.refs_1_, bf16[128,4096]{1,0:T(8,128)(2,1)S(1)} %collective-permute-done.16.refs_2_, ...), custom_call_target="tpu_custom_call" | custom-call | bytes 16777216 | tf_op jit(solution)/shard_map/place/pallas_call | solution.py:209
  138.2 14.9 %up_project.1 = (bf16[512,4096]{1,0:T(8,128)(2,1)}, bf16[512,4096]{1,0:T(8,128)(2,1)}) custom-call(bf16[512,1024]{1,0:T(8,128)(2,1)S(1)} %fusion.12.rows_ref.left_ref, bf16[1024,4096]{1,0:T(8,128)(2,1)} %place.6.weight_ref, f32[1,4096]{1,0:T(1,128)S(1)} %maximum_convert_fusion.1.bias_ref), custom_call_target="tpu_custom_call" | custom-call | flops 15000000512 | bytes 17825792 | tf_op jit(solution)/shard_map/up_project/pallas_call | solution.py:185
  157.0 7.1 %place.7 = bf16[4096,1024]{1,0:T(8,128)(2,1)} custom-call(s32[6]{0:T(128)S(1)} %stack.395.place_ref, bf16[1024,1024]{1,0:T(8,128)(2,1)} %refs_0_.5, bf16[512,1024]{1,0:T(8,128)(2,1)S(1)} %collective-permute-done.20.refs_1_, bf16[512,1024]{1,0:T(8,128)(2,1)S(1)} %collective-permute-done.21.refs_2_, bf16[1024,1024]{1,0:T(8,128)(2,1)} %collective-permute-done.22.refs_3_, ...), custom_call_target="tpu_custom_call" | custom-call | bytes 16777216 | tf_op jit(solution)/shard_map/place/pallas_call | solution.py:209
  164.1 8.7 %fusion.33 = (f32[512]{0:T(512)S(1)}, f32[512,1024]{1,0:T(8,128)S(1)}) fusion(f32[1024]{0:T(1024)S(1)} %maximum_convert_fusion.7, bf16[512,4096]{1,0:T(8,128)(2,1)S(1)} %copy-done.5, bf16[4096,1024]{1,0:T(8,128)(2,1)} %place.7, f32[1024]{0:T(1024)S(1)} %maximum_convert_fusion.6, f32[1024]{0:T(1024)S(1)} %maximum_convert_fusion.5, ...), kind=kOutput, calls=%fused_computation.212 | convolution fusion | flops 4298636800 | bytes 16795648 | tf_op jit(solution)/shard_map/dot_general | solution.py:258
  179.1 9.5 %convert_reduce_fusion = (f32[4096]{0:T(1024)S(1)}, bf16[512,4096]{1,0:T(8,128)(2,1)}) fusion(bf16[512,4096]{1,0:T(8,128)(2,1)S(1)} %copy-done.31, bf16[512,1024]{1,0:T(8,128)(2,1)S(1)} %get-tuple-element.95.right_ref, bf16[4096,1024]{1,0:T(8,128)(2,1)} %place.7), kind=kOutput, calls=%fused_computation | convolution fusion | flops 4305448960 | bytes 17842176 | tf_op jit(solution)/shard_map/dot_general | solution.py:262
  197.6 10.4 %multiply_reduce_fusion.1 = (f32[1024]{0:T(1024)S(1)}, f32[512]{0:T(512)S(1)}, f32[512]{0:T(512)S(1)}, f32[1024]{0:T(1024)S(1)}, f32[512,1024]{1,0:T(8,128)S(1)}) fusion(f32[512,1024]{1,0:T(8,128)S(1)} %copy-done.10, f32[512]{0:T(512)S(1)} %add_rsqrt_fusion.1, f32[512]{0:T(512)S(1)} %broadcast_multiply_fusion.5, f32[1024]{0:T(1024)S(1)} %maximum_convert_fusion.5, ...), kind=kOutput, calls=%fused_computation.19 | convolution fusion | flops 4306498560 | bytes 19955716 | tf_op jit(solution)/shard_map/dot_general | solution.py:262
  227.8 14.1 %collective-permute-done.34 = bf16[512,1024]{1,0:T(8,128)(2,1)S(1)} collective-permute-done((bf16[512,1024]{1,0:T(8,128)(2,1)S(1)}, bf16[512,1024]{1,0:T(8,128)(2,1)S(1)}, u32[]{:S(2)}, u32[]{:S(2)}) %collective-permute-start.34) | collective-permute-done | bytes 1048608 | tf_op jit(solution)/shard_map/ppermute | solution.py:309
  257.9 5.6 collective-permute-done.30
  269.6 9.9 %collective-permute-done.57 = bf16[64,1024]{1,0:T(8,128)(2,1)S(1)} collective-permute-done((bf16[64,1024]{1,0:T(8,128)(2,1)S(1)}, bf16[64,1024]{1,0:T(8,128)(2,1)S(1)}, u32[]{:S(2)}, u32[]{:S(2)}) %collective-permute-start.57) | collective-permute-done | bytes 131104 | tf_op jit(solution)/shard_map/ppermute | solution.py:309
  282.7 10.9 %collective-permute-done.58 = bf16[64,1024]{1,0:T(8,128)(2,1)S(1)} collective-permute-done((bf16[64,1024]{1,0:T(8,128)(2,1)S(1)}, bf16[64,1024]{1,0:T(8,128)(2,1)S(1)}, u32[]{:S(2)}, u32[]{:S(2)}) %collective-permute-start.58) | collective-permute-done | bytes 131104 | tf_op jit(solution)/shard_map/ppermute | solution.py:309
  309.2 15.6 %attend_back.2 = (bf16[512,512]{1,0:T(8,128)(2,1)S(1)}, f32[512,512]{1,0:T(8,128)S(1)}, bf16[512,512]{1,0:T(8,128)(2,1)S(1)}, f32[512,512]{1,0:T(8,128)S(1)}, bf16[512,512]{1,0:T(8,128)(2,1)S(1)}) custom-call(bf16[512,1024]{1,0:T(8,128)(2,1)} %copy-done.4, bf16[512,1024]{1,0:T(8,128)(2,1)} %copy-done.3, bf16[512,1024]{1,0:T(8,128)(2,1)} %collective-permute-done.8.k2_ref, ...), custom_call_target="tpu_custom_call" | custom-call | flops 16000000000 | bytes 8388608 | tf_op jit(solution)/shard_map/attend_back/pallas_call | solution.py:134
  324.8 15.3 %attend_back.3 = (bf16[512,512]{1,0:T(8,128)(2,1)S(1)}, f32[512,512]{1,0:T(8,128)S(1)}, bf16[512,512]{1,0:T(8,128)(2,1)S(1)}, f32[512,512]{1,0:T(8,128)S(1)}, bf16[512,512]{1,0:T(8,128)(2,1)S(1)}) custom-call(bf16[512,1024]{1,0:T(8,128)(2,1)} %copy-done.4, bf16[512,1024]{1,0:T(8,128)(2,1)} %copy-done.3, bf16[512,1024]{1,0:T(8,128)(2,1)} %collective-permute-done.8.k2_ref, ...), custom_call_target="tpu_custom_call" | custom-call | flops 16000000000 | bytes 8388608 | tf_op jit(solution)/shard_map/attend_back/pallas_call | solution.py:134
  358.5 17.0 %collective-permute-done.67 = bf16[512,1024]{1,0:T(8,128)(2,1)S(1)} collective-permute-done((bf16[512,1024]{1,0:T(8,128)(2,1)S(1)}, bf16[512,1024]{1,0:T(8,128)(2,1)S(1)}, u32[]{:S(2)}, u32[]{:S(2)}) %collective-permute-start.67) | collective-permute-done | bytes 1048608 | tf_op jit(solution)/shard_map/ppermute | solution.py:309
  377.5 19.5 %collective-permute-done.61 = bf16[512,1024]{1,0:T(8,128)(2,1)S(1)} collective-permute-done((bf16[512,1024]{1,0:T(8,128)(2,1)S(1)}, bf16[512,1024]{1,0:T(8,128)(2,1)S(1)}, u32[]{:S(2)}, u32[]{:S(2)}) %collective-permute-start.61) | collective-permute-done | bytes 1048608 | tf_op jit(solution)/shard_map/ppermute | solution.py:309
  403.9 8.3 %collective-permute-done.62 = bf16[256,1024]{1,0:T(8,128)(2,1)S(1)} collective-permute-done((bf16[256,1024]{1,0:T(8,128)(2,1)S(1)}, bf16[256,1024]{1,0:T(8,128)(2,1)S(1)}, u32[]{:S(2)}, u32[]{:S(2)}) %collective-permute-start.62) | collective-permute-done | bytes 524320 | tf_op jit(solution)/shard_map/ppermute | solution.py:309
  426.5 14.6 %collective-permute-done.70 = bf16[128,1024]{1,0:T(8,128)(2,1)S(1)} collective-permute-done((bf16[128,1024]{1,0:T(8,128)(2,1)S(1)}, bf16[128,1024]{1,0:T(8,128)(2,1)S(1)}, u32[]{:S(2)}, u32[]{:S(2)}) %collective-permute-start.70) | collective-permute-done | bytes 262176 | tf_op jit(solution)/shard_map/ppermute | solution.py:309
  470.0 8.2 %collective-permute-done.66 = bf16[256,1024]{1,0:T(8,128)(2,1)S(1)} collective-permute-done((bf16[256,1024]{1,0:T(8,128)(2,1)S(1)}, bf16[256,1024]{1,0:T(8,128)(2,1)S(1)}, u32[]{:S(2)}, u32[]{:S(2)}) %collective-permute-start.66) | collective-permute-done | bytes 524320 | tf_op jit(solution)/shard_map/ppermute | solution.py:309
  489.9 5.6 copy.38
  515.4 8.9 %collective-permute-done.44 = bf16[256,1024]{1,0:T(8,128)(2,1)S(1)} collective-permute-done((bf16[256,1024]{1,0:T(8,128)(2,1)S(1)}, bf16[256,1024]{1,0:T(8,128)(2,1)S(1)}, u32[]{:S(2)}, u32[]{:S(2)}) %collective-permute-start.44) | collective-permute-done | bytes 524320 | tf_op jit(solution)/shard_map/ppermute | solution.py:309
  556.9 7.8 %collective-permute-done.48 = bf16[256,1024]{1,0:T(8,128)(2,1)S(1)} collective-permute-done((bf16[256,1024]{1,0:T(8,128)(2,1)S(1)}, bf16[256,1024]{1,0:T(8,128)(2,1)S(1)}, u32[]{:S(2)}, u32[]{:S(2)}) %collective-permute-start.48) | collective-permute-done | bytes 524320 | tf_op jit(solution)/shard_map/ppermute | solution.py:309
  (421 shorter events, 283.6 us)
Async XLA Ops:
  13.4 32.0 %collective-permute-start = (bf16[256,1024]{1,0:T(8,128)(2,1)}, bf16[256,1024]{1,0:T(8,128)(2,1)}, u32[]{:S(2)}, u32[]{:S(2)}) collective-permute-start(bf16[256,1024]{1,0:T(8,128)(2,1)} %get-tuple-element.131), channel_id=1, source_target_pairs={{0,2},{1,3},{2,0},{3,1},{4,6},{5,7},{6,4},{7,5},{8,10},{9,11},{10,... | collective-permute-start | bytes 1572872 | tf_op jit(solution)/shard_map/ppermute | solution.py:309
  13.6 62.7 %collective-permute-start.3 = (bf16[256,3072]{1,0:T(8,128)(2,1)S(1)}, bf16[256,3072]{1,0:T(8,128)(2,1)}, u32[]{:S(2)}, u32[]{:S(2)}) collective-permute-start(bf16[256,3072]{1,0:T(8,128)(2,1)S(1)} %constant_dynamic-update-slice_fusion.refs_0_), channel_id=1, source_target_pairs={{0,1},{1,0},{2,3},{3,2},{4,5},{5,4},{6,7},{7,6},{8,9},{9,8},{10,11... | collective-permute-start | bytes 4718600 | tf_op jit(solution)/shard_map/ppermute | solution.py:309
  14.6 29.2 %collective-permute-start.1 = (bf16[128,3072]{1,0:T(8,128)(2,1)}, bf16[128,3072]{1,0:T(8,128)(2,1)S(1)}, u32[]{:S(2)}, u32[]{:S(2)}) collective-permute-start(bf16[128,3072]{1,0:T(8,128)(2,1)} %constant_dynamic-slice_fusion.16), channel_id=1, source_target_pairs={{0,2},{1,3},{2,0},{3,1},{4,6},{5,7},{6,4},{7,5},{8,10},{9,11},{10,... | collective-permute-start | bytes 2359304 | tf_op jit(solution)/shard_map/ppermute | solution.py:309
  45.4 29.3 %collective-permute-start.15 = (bf16[128,4096]{1,0:T(8,128)(2,1)}, bf16[128,4096]{1,0:T(8,128)(2,1)S(1)}, u32[]{:S(2)}, u32[]{:S(2)}) collective-permute-start(bf16[128,4096]{1,0:T(8,128)(2,1)} %constant_dynamic-slice_fusion.14), channel_id=1, source_target_pairs={{0,2},{1,3},{2,0},{3,1},{4,6},{5,7},{6,4},{7,5},{8,10},{9,11},{10,... | collective-permute-start | bytes 3145736 | tf_op jit(solution)/shard_map/ppermute | solution.py:309
  46.1 30.4 %collective-permute-start.4 = (bf16[128,3072]{1,0:T(8,128)(2,1)S(1)}, bf16[128,3072]{1,0:T(8,128)(2,1)S(1)}, u32[]{:S(2)}, u32[]{:S(2)}) collective-permute-start(bf16[128,3072]{1,0:T(8,128)(2,1)S(1)} %collective-permute-done.1.refs_1_), channel_id=1, source_target_pairs={{0,1},{1,0},{2,3},{3,2},{4,5},{5,4},{6,7},{7,6},{8,9},{9,8},{10,11... | collective-permute-start | bytes 2359304 | tf_op jit(solution)/shard_map/ppermute | solution.py:309
  93.9 34.9 %collective-permute-start.17 = (bf16[256,4096]{1,0:T(8,128)(2,1)S(1)}, bf16[256,4096]{1,0:T(8,128)(2,1)}, u32[]{:S(2)}, u32[]{:S(2)}) collective-permute-start(bf16[256,4096]{1,0:T(8,128)(2,1)S(1)} %copy-done.14), channel_id=1, source_target_pairs={{0,1},{1,0},{2,3},{3,2},{4,5},{5,4},{6,7},{7,6},{8,9},{9,8},{10,11... | collective-permute-start | bytes 6291464 | tf_op jit(solution)/shard_map/ppermute | solution.py:309
  101.9 55.1 %collective-permute-start.22 = (bf16[1024,1024]{1,0:T(8,128)(2,1)}, bf16[1024,1024]{1,0:T(8,128)(2,1)}, u32[]{:S(2)}, u32[]{:S(2)}) collective-permute-start(bf16[1024,1024]{1,0:T(8,128)(2,1)} %refs_0_.5), channel_id=1, source_target_pairs={{0,1},{1,0},{2,3},{3,2},{4,5},{5,4},{6,7},{7,6},{8,9},{9,8},{10,11... | collective-permute-start | bytes 6291464 | tf_op jit(solution)/shard_map/ppermute | solution.py:309
  128.8 44.4 %collective-permute-start.25 = (bf16[256,1024]{1,0:T(8,128)(2,1)}, bf16[256,1024]{1,0:T(8,128)(2,1)}, u32[]{:S(2)}, u32[]{:S(2)}) collective-permute-start(bf16[256,1024]{1,0:T(8,128)(2,1)} %get-tuple-element.46), channel_id=1, source_target_pairs={{0,2},{1,3},{2,0},{3,1},{4,6},{5,7},{6,4},{7,5},{8,10},{9,11},{10,... | collective-permute-start | bytes 1572872 | tf_op jit(solution)/shard_map/ppermute | solution.py:309
  156.5 32.5 %collective-permute-start.26 = (bf16[512,2048]{1,0:T(8,128)(2,1)}, bf16[512,2048]{1,0:T(8,128)(2,1)S(1)}, u32[]{:S(2)}, u32[]{:S(2)}) collective-permute-start(bf16[512,2048]{1,0:T(8,128)(2,1)} %pad_maximum_fusion.1), channel_id=1, source_target_pairs={{0,1},{1,0},{2,3},{3,2},{4,5},{5,4},{6,7},{7,6},{8,9},{9,8},{10,11... | collective-permute-start | bytes 6291464 | tf_op jit(solution)/shard_map/ppermute | solution.py:309
  188.6 113.4 %collective-permute-start.32 = (bf16[512,4096]{1,0:T(8,128)(2,1)}, bf16[512,4096]{1,0:T(8,128)(2,1)}, u32[]{:S(2)}, u32[]{:S(2)}) collective-permute-start(bf16[512,4096]{1,0:T(8,128)(2,1)} %get-tuple-element.48.right_ref), channel_id=1, source_target_pairs={{0,1},{1,0},{2,3},{3,2},{4,5},{5,4},{6,7},{7,6},{8,9},{9,8},{10,11... | collective-permute-start | bytes 12582920 | tf_op jit(solution)/shard_map/ppermute | solution.py:309
  193.4 32.2 %collective-permute-start.33 = (bf16[512,1024]{1,0:T(8,128)(2,1)S(1)}, bf16[512,1024]{1,0:T(8,128)(2,1)}, u32[]{:S(2)}, u32[]{:S(2)}) collective-permute-start(bf16[512,1024]{1,0:T(8,128)(2,1)S(1)} %grad_rows.14), channel_id=1, source_target_pairs={{0,2},{1,3},{2,0},{3,1},{4,6},{5,7},{6,4},{7,5},{8,10},{9,11},{10,... | collective-permute-start | bytes 3145736 | tf_op jit(solution)/shard_map/ppermute | solution.py:309
  210.9 31.0 %collective-permute-start.34 = (bf16[512,1024]{1,0:T(8,128)(2,1)S(1)}, bf16[512,1024]{1,0:T(8,128)(2,1)S(1)}, u32[]{:S(2)}, u32[]{:S(2)}) collective-permute-start(bf16[512,1024]{1,0:T(8,128)(2,1)S(1)} %grad_rows.15), channel_id=1, source_target_pairs={{0,2},{1,3},{2,0},{3,1},{4,6},{5,7},{6,4},{7,5},{8,10},{9,11},{10,... | collective-permute-start | bytes 3145736 | tf_op jit(solution)/shard_map/ppermute | solution.py:309
  223.5 29.7 %collective-permute-start.55 = (bf16[256,1024]{1,0:T(8,128)(2,1)S(1)}, bf16[256,1024]{1,0:T(8,128)(2,1)S(1)}, u32[]{:S(2)}, u32[]{:S(2)}) collective-permute-start(bf16[256,1024]{1,0:T(8,128)(2,1)S(1)} %grad_rows.16), channel_id=1, source_target_pairs={{0,2},{1,3},{2,0},{3,1},{4,6},{5,7},{6,4},{7,5},{8,10},{9,11},{10,... | collective-permute-start | bytes 1572872 | tf_op jit(solution)/shard_map/ppermute | solution.py:309
  224.3 39.3 %collective-permute-start.30 = (bf16[256,1024]{1,0:T(8,128)(2,1)}, bf16[256,1024]{1,0:T(8,128)(2,1)S(1)}, u32[]{:S(2)}, u32[]{:S(2)}) collective-permute-start(bf16[256,1024]{1,0:T(8,128)(2,1)} %get-tuple-element.49), channel_id=1, source_target_pairs={{0,2},{1,3},{2,0},{3,1},{4,6},{5,7},{6,4},{7,5},{8,10},{9,11},{10,... | collective-permute-start | bytes 1572872 | tf_op jit(solution)/shard_map/ppermute | solution.py:309
  253.2 48.7 %collective-permute-start.31 = (bf16[512,512]{1,0:T(8,128)(2,1)S(1)}, bf16[512,512]{1,0:T(8,128)(2,1)S(1)}, u32[]{:S(2)}, u32[]{:S(2)}) collective-permute-start(bf16[512,512]{1,0:T(8,128)(2,1)S(1)} %pad_maximum_fusion.8), channel_id=1, source_target_pairs={{0,1},{1,0},{2,3},{3,2},{4,5},{5,4},{6,7},{7,6},{8,9},{9,8},{10,11... | collective-permute-start | bytes 1572872 | tf_op jit(solution)/shard_map/ppermute | solution.py:309
  293.8 55.6 %collective-permute-start.80 = (bf16[128,1024]{1,0:T(8,128)(2,1)S(1)}, bf16[128,1024]{1,0:T(8,128)(2,1)S(1)}, u32[]{:S(2)}, u32[]{:S(2)}) collective-permute-start(bf16[128,1024]{1,0:T(8,128)(2,1)S(1)} %add_convert_fusion.13), channel_id=1, source_target_pairs={{0,8},{4,12},{8,0},{12,4},{16,24},{20,28},{24,16},{28,20},{1,9},{5... | collective-permute-start | bytes 786440 | tf_op jit(solution)/shard_map/ppermute | solution.py:309
  298.6 52.2 %collective-permute-start.75 = (bf16[128,1024]{1,0:T(8,128)(2,1)S(1)}, bf16[128,1024]{1,0:T(8,128)(2,1)}, u32[]{:S(2)}, u32[]{:S(2)}) collective-permute-start(bf16[128,1024]{1,0:T(8,128)(2,1)S(1)} %add_convert_fusion.17), channel_id=1, source_target_pairs={{0,8},{4,12},{8,0},{12,4},{16,24},{20,28},{24,16},{28,20},{1,9},{5... | collective-permute-start | bytes 786440 | tf_op jit(solution)/shard_map/ppermute | solution.py:309
  301.3 51.5 %collective-permute-start.60 = (bf16[128,1024]{1,0:T(8,128)(2,1)S(1)}, bf16[128,1024]{1,0:T(8,128)(2,1)S(1)}, u32[]{:S(2)}, u32[]{:S(2)}) collective-permute-start(bf16[128,1024]{1,0:T(8,128)(2,1)S(1)} %bitcast.165), channel_id=1, source_target_pairs={{0,4},{4,0},{8,12},{12,8},{16,20},{20,16},{24,28},{28,24},{1,5},{5... | collective-permute-start | bytes 786440 | tf_op jit(solution)/shard_map/ppermute | solution.py:309
  350.8 46.3 %collective-permute-start.61 = (bf16[512,1024]{1,0:T(8,128)(2,1)S(1)}, bf16[512,1024]{1,0:T(8,128)(2,1)S(1)}, u32[]{:S(2)}, u32[]{:S(2)}) collective-permute-start(bf16[512,1024]{1,0:T(8,128)(2,1)S(1)} %grad_rows.17), channel_id=1, source_target_pairs={{0,2},{1,3},{2,0},{3,1},{4,6},{5,7},{6,4},{7,5},{8,10},{9,11},{10,... | collective-permute-start | bytes 3145736 | tf_op jit(solution)/shard_map/ppermute | solution.py:309
  352.8 61.0 %collective-permute-start.81 = (bf16[256,1024]{1,0:T(8,128)(2,1)S(1)}, bf16[256,1024]{1,0:T(8,128)(2,1)S(1)}, u32[]{:S(2)}, u32[]{:S(2)}) collective-permute-start(bf16[256,1024]{1,0:T(8,128)(2,1)S(1)} %bitcast.152), channel_id=1, source_target_pairs={{0,4},{4,0},{8,12},{12,8},{16,20},{20,16},{24,28},{28,24},{1,5},{5... | collective-permute-start | bytes 1572872 | tf_op jit(solution)/shard_map/ppermute | solution.py:309
  355.5 67.7 %collective-permute-start.76 = (bf16[256,1024]{1,0:T(8,128)(2,1)S(1)}, bf16[256,1024]{1,0:T(8,128)(2,1)S(1)}, u32[]{:S(2)}, u32[]{:S(2)}) collective-permute-start(bf16[256,1024]{1,0:T(8,128)(2,1)S(1)} %bitcast.150), channel_id=1, source_target_pairs={{0,4},{4,0},{8,12},{12,8},{16,20},{20,16},{24,28},{28,24},{1,5},{5... | collective-permute-start | bytes 1572872 | tf_op jit(solution)/shard_map/ppermute | solution.py:309
  358.4 106.5 %collective-permute-start.39 = (bf16[512,3072]{1,0:T(8,128)(2,1)S(1)}, bf16[512,3072]{1,0:T(8,128)(2,1)}, u32[]{:S(2)}, u32[]{:S(2)}) collective-permute-start(bf16[512,3072]{1,0:T(8,128)(2,1)S(1)} %pad_maximum_fusion.right_ref), channel_id=1, source_target_pairs={{0,1},{1,0},{2,3},{3,2},{4,5},{5,4},{6,7},{7,6},{8,9},{9,8},{10,11... | collective-permute-start | bytes 9437192 | tf_op jit(solution)/shard_map/ppermute | solution.py:309
  416.3 48.6 %collective-permute-start.38 = (bf16[512,512]{1,0:T(8,128)(2,1)S(1)}, bf16[512,512]{1,0:T(8,128)(2,1)S(1)}, u32[]{:S(2)}, u32[]{:S(2)}) collective-permute-start(bf16[512,512]{1,0:T(8,128)(2,1)S(1)} %copy-done.28), channel_id=1, source_target_pairs={{0,1},{1,0},{2,3},{3,2},{4,5},{5,4},{6,7},{7,6},{8,9},{9,8},{10,11... | collective-permute-start | bytes 1572872 | tf_op jit(solution)/shard_map/ppermute | solution.py:309
  468.6 39.0 %collective-permute-start.43 = (bf16[512,1024]{1,0:T(8,128)(2,1)S(1)}, bf16[512,1024]{1,0:T(8,128)(2,1)}, u32[]{:S(2)}, u32[]{:S(2)}) collective-permute-start(bf16[512,1024]{1,0:T(8,128)(2,1)S(1)} %grad_rows.21), channel_id=1, source_target_pairs={{0,2},{1,3},{2,0},{3,1},{4,6},{5,7},{6,4},{7,5},{8,10},{9,11},{10,... | collective-permute-start | bytes 3145736 | tf_op jit(solution)/shard_map/ppermute | solution.py:309
  (97 other events, 1362.6 us)
